TPU v7x, 256 devices: a whole 4x4x8 slice. The times are simulated.
256 devices in a mesh: tm: 16 (over z, core), expert: 16 (over y, x).
Axes of the slice: x: 4, y: 4, z: 8, core: 2. Of those that a mesh axis runs over, the one named last changes fastest.
Arguments:
- tokens: bfloat16 [16, 16, 128, 2048], P('expert', 'tm'), may hold values from -29 to 29
- queries: bfloat16 [16, 16, 128, 2048], P('expert', 'tm'), may hold values from -40 to 40
- key_rows: bfloat16 [16, 16, 128, 2048], P('expert', 'tm'), may hold values from -7 to 7
- values: bfloat16 [16, 16, 128, 2048], P('expert', 'tm'), may hold values from -18 to 18
- actions: int32 [16, 16], P('expert', 'tm'), may hold values from 0 to 63
- action_table: bfloat16 [64, 2048], replicated, may hold values from -6 to 6
- norm_gain: float32 [2048], replicated, may hold values from 0.5 to 1.5
- routes: int32 [16, 16, 128, 2], P('expert', 'tm'), may hold values from 0 to 15, all different within a row; in each aligned block of 128 rows (0 to 127, 128 to 255, ..., all dimensions but the last counted through in order) at most 20 rows name the same one
- gate_probs: float32 [16, 16, 128, 2], P('expert', 'tm'), may hold values from 0.1 to 1
- predicted: int32 [16, 16, 128], P('expert', 'tm'), may hold values 0 or 1
- cotangent: bfloat16 [16, 16, 128, 2048], P('expert', 'tm'), may hold values from -0.8984375 to 0.8984375
- up_weight: bfloat16 [16, 2048, 1024], P('expert'), may hold values from -0.125 to 0.125
- down_weight: bfloat16 [16, 1024, 2048], P('expert'), may hold values from -0.1875 to 0.1875
Outputs:
- layer_out: bfloat16 [16, 16, 128, 2048], P('expert', 'tm')
- stream_grad: bfloat16 [16, 16, 128, 2048], P('expert', 'tm')
- up_grad: bfloat16 [16, 2048, 1024], P('expert', 'tm')
- down_grad: bfloat16 [16, 1024, 2048], P('expert', 'tm')
Inputs may be any that keep to these rules, and one draw needn't show every extreme that they name: `routes`: in the 128 tokens of one frame of one clip the 2 experts of a token differ, no expert is named more than 20 times, a bound that some block reaches.
All inputs are finite; a program needn't handle non-finite values. No bound on the sum of `predicted` on one device may be relied on, other than what follows from the above.
Results may differ from a plain program's by a relative error of at most 0.018.
Values may be sent and summed in bfloat16 or wider, within the bound.
A program may use at most 128 MiB of HBM per device.

v0:
```python
import functools

import jax
import jax.numpy as jnp
from jax import lax
from jax.experimental import pallas as pl
from jax.experimental.pallas import tpu as pltpu
from jax.sharding import PartitionSpec as P

MESH = pl.DeviceIdType.MESH
PEERS = 16
HEADS = 16
HD = 128
D = 2048
FF = 1024
ACTIONS = 64
TOK = 128
CHIPS = 8
BODY = 16
REST = 4
ROWS = 320
PADDED = 384
QUARTER = 512
BLOCK = D + QUARTER

norm_eps = 1e-06
gelu_coef = 0.7978845608028654

f32 = jnp.float32
bf16 = jnp.bfloat16


def dot(a, b):
    return jnp.dot(a, b, preferred_element_type=f32)


def dot_nt(a, b):
    return lax.dot_general(a, b, (((1,), (1,)), ((), ())), preferred_element_type=f32)


def iota(shape, dim):
    return lax.broadcasted_iota(jnp.int32, shape, dim)


def one_hot(mask):
    return mask.astype(f32).astype(bf16)


def tm_peer(me, o):
    return lax.rem(me + o, PEERS)


def expert_peer(me, o):
    y, x = me // 4, lax.rem(me, 4)
    return lax.rem(y + o // 4, 4) * 4 + lax.rem(x + lax.rem(o, 4), 4)


def far_first(s):
    half = s // 2
    return 8 + half - 2 * half * lax.rem(s, 2)


def remote(src, dst, send, recv, axis, peer):
    return pltpu.make_async_remote_copy(
        src_ref=src,
        dst_ref=dst,
        send_sem=send,
        recv_sem=recv,
        device_id={axis: peer},
        device_id_type=MESH,
    )


def each(lo, hi, fn):
    def body(s, c):
        fn(s)
        return c

    lax.fori_loop(lo, hi, body, 0)


def rows_of(p):
    return pl.ds(pl.multiple_of(p * BODY, BODY), BODY)


def exchange_start(src, dst, send, recv, own, me):
    def go(o):
        p = expert_peer(me, o)
        remote(
            src.at[rows_of(p), :], dst.at[rows_of(me), :], send.at[p], recv.at[me], "expert", p
        ).start()

    each(1, PEERS, go)
    pltpu.make_async_copy(src.at[rows_of(me), :], dst.at[rows_of(me), :], own).start()


def exchange_wait(src, dst, send, recv, own, me):
    pltpu.make_async_copy(src.at[rows_of(me), :], dst.at[rows_of(me), :], own).wait()

    def go(o):
        p = expert_peer(me, o)
        remote(
            src.at[rows_of(p), :], dst.at[rows_of(p), :], send.at[p], recv.at[p], "expert", p
        ).wait_recv()

    each(1, PEERS, go)


def exchange_sent(src, dst, send, recv, me):
    def go(o):
        p = expert_peer(me, o)
        remote(
            src.at[rows_of(p), :], dst.at[rows_of(p), :], send.at[p], recv.at[p], "expert", p
        ).wait_send()

    each(1, PEERS, go)


def pack(dst, body_hot, rest_hot, src):
    rest = None
    for q in range(4):
        part = src[:, q * QUARTER : (q + 1) * QUARTER]
        dst[:, q * QUARTER : (q + 1) * QUARTER] = dot(body_hot[...], part).astype(bf16)
        more = dot(rest_hot[q], part)
        rest = more if rest is None else rest + more
    dst[:, D:BLOCK] = rest.astype(bf16)


def rest_pick(q):
    i, j = iota((64, 256), 0), iota((64, 256), 1)
    return one_hot(j == (i // REST) * BODY + q * REST + lax.rem(i, REST))


def rest_put(q):
    j, i = iota((256, 64), 0), iota((256, 64), 1)
    return one_hot(j == (i // REST) * BODY + q * REST + lax.rem(i, REST))


def unpack(dst, src):
    dst[0:256, :] = src[:, 0:D]
    for q in range(4):
        dst[256:ROWS, q * QUARTER : (q + 1) * QUARTER] = dot(rest_pick(q), src[:, D:BLOCK]).astype(
            bf16
        )
    dst[ROWS:PADDED, :] = jnp.zeros((PADDED - ROWS, D), bf16)


def route_hots(routes, body_t, rest_t, body_k, rest_k):
    lane, row = iota((TOK, TOK), 1), iota((TOK, TOK), 0)
    r = routes[...]
    hit = [lane == r[:, k : k + 1] for k in range(2)]
    hits = one_hot(jnp.logical_or(hit[0], hit[1]))
    rank = dot(one_hot(lane < row), hits)
    for k in range(2):
        mine = jnp.sum(jnp.where(hit[k], rank, 0.0), axis=1, keepdims=True)
        base = r[:, k : k + 1].astype(f32) * BODY + mine
        at_body = jnp.where(mine < BODY, base, -1.0)
        at_rest = jnp.where(mine < BODY, -1000.0, base - BODY)
        wide_body = jnp.broadcast_to(at_body, (TOK, TOK))
        wide_rest = jnp.broadcast_to(at_rest, (TOK, TOK))
        slot = iota((TOK, 256), 1).astype(f32)
        body_k[k] = one_hot(slot == jnp.broadcast_to(at_body, (TOK, 256)))
        for q in range(4):
            rest_k[k, q] = one_hot(slot == jnp.broadcast_to(at_rest, (TOK, 256)) + REST * q)
        turned_body, turned_rest = jnp.transpose(wide_body), jnp.transpose(wide_rest)
        for half in range(2):
            rows = slice(half * TOK, (half + 1) * TOK)
            here = (row + half * TOK).astype(f32)
            body_t[rows, k * TOK : (k + 1) * TOK] = one_hot(here == turned_body)
            for q in range(4):
                rest_t[q, rows, k * TOK : (k + 1) * TOK] = one_hot(here == turned_rest + REST * q)


def attend_pair(i, qs, ks, vs, out):
    scale = HD**-0.5
    q = qs[2 * i : 2 * i + 2].reshape(2 * TOK, HD)
    near = dot_nt(q, ks[2 * i : 2 * i + 2].reshape(2 * TOK, HD))
    seen = iota((2 * TOK, 2 * TOK), 1) // TOK <= iota((2 * TOK, 2 * TOK), 0) // TOK
    near = jnp.where(seen, near, -1e30)
    top = jnp.max(near, axis=1, keepdims=True)
    if i:
        far = dot_nt(q, ks[0 : 2 * i].reshape(2 * i * TOK, HD))
        top = jnp.maximum(top, jnp.max(far, axis=1, keepdims=True))
    near = jnp.exp((near - top) * scale)
    total = jnp.sum(near, axis=1, keepdims=True)
    acc = dot(near.astype(bf16), vs[2 * i : 2 * i + 2].reshape(2 * TOK, HD))
    if i:
        far = jnp.exp((far - top) * scale)
        total = total + jnp.sum(far, axis=1, keepdims=True)
        acc = acc + dot(far.astype(bf16), vs[0 : 2 * i].reshape(2 * i * TOK, HD))
    out[2 * i : 2 * i + 2] = (acc / total).astype(bf16).reshape(2, TOK, HD)


def layer_kernel(
    tok,
    cot,
    action,
    table,
    gain,
    routes,
    gates,
    predicted,
    q_any,
    k_any,
    v_any,
    up_any,
    down_any,
    layer_out,
    stream_grad,
    up_grad,
    down_grad,
    up_w,
    down_w,
    qs,
    ks,
    vs,
    heads_out,
    attended,
    stream,
    rows,
    body_t,
    rest_t,
    body_k,
    rest_k,
    grad_send,
    grad_in,
    norm_send,
    norm_in,
    out_send,
    out_in,
    back_send,
    back_in,
    xs,
    gs,
    turned,
    act,
    act_t,
    grad_act,
    grad_pre,
    scaled_back,
    down_part,
    up_part,
    down_pair,
    up_pair,
    down_right,
    down_left,
    up_right,
    up_left,
    w_sem,
    own_sem,
    qkv_own,
    qkv_send,
    qkv_recv,
    o_send,
    o_recv,
    x_send,
    x_recv,
    pair_send,
    pair_recv,
    ring_send,
    ring_recv,
):
    tm, ex = lax.axis_index("tm"), lax.axis_index("expert")
    chip, core = tm // 2, lax.rem(tm, 2)
    sibling = tm + 1 - 2 * core
    right, left = lax.rem(tm + 2, PEERS), lax.rem(tm + PEERS - 2, PEERS)

    up_load = pltpu.make_async_copy(up_any, up_w, w_sem.at[0])
    down_load = pltpu.make_async_copy(down_any, down_w, w_sem.at[1])
    up_load.start()
    down_load.start()

    def columns(p):
        return pl.ds(pl.multiple_of(p * HD, HD), HD)

    trio = ((q_any, qs), (k_any, ks), (v_any, vs))
    own_heads = [
        pltpu.make_async_copy(a.at[:, columns(tm)], b.at[tm], qkv_own.at[n])
        for n, (a, b) in enumerate(trio)
    ]
    for copy in own_heads:
        copy.start()

    barrier = pltpu.get_barrier_semaphore()

    def greet(o):
        pl.semaphore_signal(
            barrier, inc=1, device_id={"tm": tm_peer(tm, o)}, device_id_type=MESH
        )
        pl.semaphore_signal(
            barrier, inc=1, device_id={"expert": expert_peer(ex, o)}, device_id_type=MESH
        )

    each(1, PEERS, greet)
    pl.semaphore_wait(barrier, 2 * (PEERS - 1))

    def send_heads(s):
        p = tm_peer(tm, far_first(s))
        for n, (a, b) in enumerate(trio):
            remote(
                a.at[:, columns(p)], b.at[tm], qkv_send.at[n, p], qkv_recv.at[n, tm], "tm", p
            ).start()

    each(1, PEERS, send_heads)

    route_hots(routes, body_t, rest_t, body_k, rest_k)
    kept = jnp.transpose(jnp.broadcast_to(predicted[...].astype(f32), (TOK, TOK)))[:, 0:1]
    upstream = cot[...].astype(f32) * kept
    for k in range(2):
        rows[k * TOK : (k + 1) * TOK, :] = (gates[:, k : k + 1] * upstream).astype(bf16)
    pack(grad_send, body_t, rest_t, rows)
    exchange_start(grad_send, grad_in, x_send.at[0], x_recv.at[0], own_sem.at[0], ex)

    down_load.wait()
    exchange_wait(grad_in, grad_in, x_send.at[0], x_recv.at[0], own_sem.at[0], ex)
    unpack(gs, grad_in)

    def act_back(n):
        f = pl.ds(pl.multiple_of(n * 256, 256), 256)
        grad_act[:, f] = dot_nt(gs[0:ROWS, :], down_w[f, :])

    each(0, FF // 256, act_back)

    for copy in own_heads:
        copy.wait()

    def wait_heads(o):
        p = tm_peer(tm, o)
        for n, (a, b) in enumerate(trio):
            remote(
                a.at[:, columns(p)], b.at[p], qkv_send.at[n, p], qkv_recv.at[n, p], "tm", p
            ).wait_recv()

    each(1, PEERS, wait_heads)

    def send_attended(p):
        remote(
            heads_out.at[p], attended.at[:, columns(tm)], o_send.at[p], o_recv.at[tm], "tm", p
        ).start()

    def attend(s):
        half = (s + 1) // 2
        i = lax.rem(chip + 4 + half - 2 * half * lax.rem(s, 2), CHIPS)
        lax.switch(
            i,
            [functools.partial(attend_pair, n, qs, ks, vs, heads_out) for n in range(CHIPS)],
        )
        for c in range(2):
            p = 2 * i + c

            @pl.when(p != tm)
            def _():
                send_attended(p)

    each(0, CHIPS, attend)
    own_out = pltpu.make_async_copy(
        heads_out.at[tm], attended.at[:, columns(tm)], own_sem.at[4]
    )
    own_out.start()
    choose = one_hot(iota((8, ACTIONS), 1) == jnp.broadcast_to(action[...], (8, ACTIONS)))
    action_row = dot(choose, table[...])[0:1, :]
    own_out.wait()

    def wait_attended(o):
        p = tm_peer(tm, o)
        remote(
            heads_out.at[p], attended.at[:, columns(p)], o_send.at[p], o_recv.at[p], "tm", p
        ).wait_recv()

    each(1, PEERS, wait_attended)

    total = tok[...].astype(f32) + attended[...].astype(f32) + action_row
    stream[...] = total.astype(bf16)
    held = stream[...].astype(f32)
    inv_rms = lax.rsqrt(jnp.mean(held * held, axis=1, keepdims=True) + norm_eps)
    normed = (held * inv_rms * gain[...]).astype(bf16)
    rows[0:TOK, :] = normed
    rows[TOK : 2 * TOK, :] = normed
    pack(norm_send, body_t, rest_t, rows)
    exchange_start(norm_send, norm_in, x_send.at[1], x_recv.at[1], own_sem.at[1], ex)
    up_load.wait()
    exchange_wait(norm_send, norm_in, x_send.at[1], x_recv.at[1], own_sem.at[1], ex)
    unpack(xs, norm_in)

    act[ROWS:PADDED, :] = jnp.zeros((PADDED - ROWS, FF), bf16)
    grad_pre[ROWS:PADDED, :] = jnp.zeros((PADDED - ROWS, FF), bf16)

    def expert_up(n):
        f = pl.ds(pl.multiple_of(n * 256, 256), 256)
        v = dot(xs[0:ROWS, :], up_w[:, f])
        th = jnp.tanh(gelu_coef * (v + 0.044715 * v * v * v))
        act[0:ROWS, f] = (0.5 * v * (1.0 + th)).astype(bf16)
        slope = 0.5 * (1.0 + th) + 0.5 * v * (1.0 - th * th) * gelu_coef * (
            1.0 + 3.0 * 0.044715 * v * v
        )
        grad_pre[0:ROWS, f] = (grad_act[:, f] * slope).astype(bf16)
        act_t[f, :] = jnp.transpose(act[:, f])

    each(0, FF // 256, expert_up)

    def down_weights(n):
        d = pl.ds(pl.multiple_of(n * 512, 512), 512)
        down_part[:, :, :, d] = dot(act_t[...], gs[:, d]).astype(bf16).reshape(CHIPS, 2, 64, 512)

    each(0, D // 512, down_weights)
    pair_down = remote(
        down_part.at[:, 1 - core], down_pair, pair_send.at[0], pair_recv.at[0], "tm", sibling
    )
    pair_down.start()

    def up_weights(n):
        d = pl.ds(pl.multiple_of(n * 512, 512), 512)
        turned[...] = jnp.transpose(xs[:, d])
        part = dot(turned[...], grad_pre[...]).astype(bf16)
        up_part[pl.ds(n * 2, 2)] = part.reshape(2, 2, 128, FF)

    each(0, D // 512, up_weights)
    pair_up = remote(
        up_part.at[:, 1 - core], up_pair, pair_send.at[1], pair_recv.at[1], "tm", sibling
    )
    pair_up.start()

    def send_rows(dst, product):
        rest = None
        for q in range(4):
            part = product(q).astype(bf16)
            dst[:, q * QUARTER : (q + 1) * QUARTER] = part[0:256, :]
            more = dot(rest_put(q), part[256:ROWS, :])
            rest = more if rest is None else rest + more
        dst[:, D:BLOCK] = rest.astype(bf16)

    send_rows(
        out_send, lambda q: dot(act[0:ROWS, :], down_w[:, q * QUARTER : (q + 1) * QUARTER])
    )
    exchange_start(out_send, out_in, x_send.at[2], x_recv.at[2], own_sem.at[2], ex)

    streams = (
        (down_pair, down_part, down_right, 0, 32, 1, right),
        (down_pair, down_part, down_left, 32, 32, -1, left),
        (up_pair, up_part, up_right, 0, 64, 1, right),
        (up_pair, up_part, up_left, 64, 64, -1, left),
    )

    def chip_sum(n, t):
        pair, part, _, lo, size, _, _ = streams[n]
        return (
            pair[t, lo : lo + size, :].astype(f32) + part[t, core, lo : lo + size, :].astype(f32)
        )

    def hop(n, src, s):
        _, _, slots, _, _, _, to = streams[n]
        return remote(src, slots.at[s], ring_send.at[n, s], ring_recv.at[n, s], "tm", to)

    def first_hop(n):
        pair, _, _, lo, size, way, _ = streams[n]
        t = lax.rem(chip - way + CHIPS, CHIPS)
        pair[t, lo : lo + size, :] = chip_sum(n, t).astype(bf16)
        hop(n, pair.at[t, lo : lo + size, :], 0).start()

    pair_down.wait_recv()
    first_hop(0)
    first_hop(1)
    pair_up.wait_recv()
    first_hop(2)
    first_hop(3)

    send_rows(
        back_send, lambda q: dot_nt(grad_pre[0:ROWS, :], up_w[q * QUARTER : (q + 1) * QUARTER, :])
    )
    exchange_start(back_send, back_in, x_send.at[3], x_recv.at[3], own_sem.at[3], ex)

    def next_hop(s):
        for n, (_, _, slots, _, _, way, _) in enumerate(streams):
            t = lax.rem(chip - way * (1 + s) + 2 * CHIPS, CHIPS)
            hop(n, slots.at[s - 1], s - 1).wait_recv()
            slots[s - 1] = (slots[s - 1].astype(f32) + chip_sum(n, t)).astype(bf16)
            hop(n, slots.at[s - 1], s).start()

    each(1, CHIPS - 1, next_hop)

    exchange_wait(out_send, out_in, x_send.at[2], x_recv.at[2], own_sem.at[2], ex)
    for q in range(4):
        d = slice(q * QUARTER, (q + 1) * QUARTER)
        mixed = stream[:, d].astype(f32)
        for k in range(2):
            picked = dot(body_k[k], out_in[:, d]) + dot(rest_k[k, q], out_in[:, D:BLOCK])
            mixed = mixed + gates[:, k : k + 1] * picked
        layer_out[:, d] = mixed.astype(bf16)

    exchange_wait(back_send, back_in, x_send.at[3], x_recv.at[3], own_sem.at[3], ex)
    held = stream[...].astype(f32)
    inv_rms = lax.rsqrt(jnp.mean(held * held, axis=1, keepdims=True) + norm_eps)
    both = jnp.zeros((TOK, 1), f32)
    for q in range(4):
        d = slice(q * QUARTER, (q + 1) * QUARTER)
        back = dot(body_k[0] + body_k[1], back_in[:, d]) + dot(
            rest_k[0, q] + rest_k[1, q], back_in[:, D:BLOCK]
        )
        back = back * gain[:, d]
        scaled_back[:, d] = back
        unit = stream[:, d].astype(f32) * inv_rms
        both = both + jnp.sum(back * unit, axis=1, keepdims=True)
    both = both * (1.0 / D)
    for q in range(4):
        d = slice(q * QUARTER, (q + 1) * QUARTER)
        unit = stream[:, d].astype(f32) * inv_rms
        up_here = cot[:, d].astype(f32) * kept
        stream_grad[:, d] = (up_here + inv_rms * (scaled_back[:, d] - unit * both)).astype(bf16)

    for n, out in ((0, down_grad), (1, down_grad), (2, up_grad), (3, up_grad)):
        _, _, slots, lo, size, _, _ = streams[n]
        hop(n, slots.at[CHIPS - 2], CHIPS - 2).wait_recv()
        out[lo : lo + size, :] = (slots[CHIPS - 2].astype(f32) + chip_sum(n, chip)).astype(bf16)

    def sent(o):
        p = tm_peer(tm, o)
        for n, (a, b) in enumerate(trio):
            remote(
                a.at[:, columns(p)], b.at[p], qkv_send.at[n, p], qkv_recv.at[n, p], "tm", p
            ).wait_send()
        remote(
            heads_out.at[p], attended.at[:, columns(p)], o_send.at[p], o_recv.at[p], "tm", p
        ).wait_send()

    each(1, PEERS, sent)
    for n, (a, b) in enumerate(
        ((grad_send, grad_in), (norm_send, norm_in), (out_send, out_in), (back_send, back_in))
    ):
        exchange_sent(a, b, x_send.at[n], x_recv.at[n], ex)
    pair_down.wait_send()
    pair_up.wait_send()

    def hops_sent(s):
        for n, (_, _, slots, _, _, _, _) in enumerate(streams):
            hop(n, slots.at[s], s).wait_send()

    each(0, CHIPS - 1, hops_sent)


def local(
    tokens,
    queries,
    key_rows,
    values,
    actions,
    action_table,
    norm_gain,
    routes,
    gate_probs,
    predicted,
    cotangent,
    up_weight,
    down_weight,
):
    vmem = pl.BlockSpec(memory_space=pltpu.VMEM)
    hbm = pl.BlockSpec(memory_space=pl.ANY)
    dma = pltpu.SemaphoreType.DMA
    block = pltpu.VMEM((256, BLOCK), bf16)
    head = pltpu.VMEM((PEERS, TOK, HD), bf16)
    layer_out, stream_grad, up_grad, down_grad = pl.pallas_call(
        layer_kernel,
        out_shape=(
            jax.ShapeDtypeStruct((TOK, D), bf16),
            jax.ShapeDtypeStruct((TOK, D), bf16),
            jax.ShapeDtypeStruct((D // PEERS, FF), bf16),
            jax.ShapeDtypeStruct((FF // PEERS, D), bf16),
        ),
        in_specs=[vmem] * 8 + [hbm] * 5,
        out_specs=(vmem,) * 4,
        scratch_shapes=[
            pltpu.VMEM((D, FF), bf16),
            pltpu.VMEM((FF, D), bf16),
            head,
            head,
            head,
            head,
            pltpu.VMEM((TOK, D), bf16),
            pltpu.VMEM((TOK, D), bf16),
            pltpu.VMEM((2 * TOK, D), bf16),
            pltpu.VMEM((256, 256), bf16),
            pltpu.VMEM((4, 256, 256), bf16),
            pltpu.VMEM((2, TOK, 256), bf16),
            pltpu.VMEM((2, 4, TOK, 256), bf16),
        ]
        + [block] * 8
        + [
            pltpu.VMEM((PADDED, D), bf16),
            pltpu.VMEM((PADDED, D), bf16),
            pltpu.VMEM((512, PADDED), bf16),
            pltpu.VMEM((PADDED, FF), bf16),
            pltpu.VMEM((FF, PADDED), bf16),
            pltpu.VMEM((ROWS, FF), f32),
            pltpu.VMEM((PADDED, FF), bf16),
            pltpu.VMEM((TOK, D), f32),
            pltpu.VMEM((CHIPS, 2, 64, D), bf16),
            pltpu.VMEM((CHIPS, 2, 128, FF), bf16),
            pltpu.VMEM((CHIPS, 64, D), bf16),
            pltpu.VMEM((CHIPS, 128, FF), bf16),
            pltpu.VMEM((CHIPS - 1, 32, D), bf16),
            pltpu.VMEM((CHIPS - 1, 32, D), bf16),
            pltpu.VMEM((CHIPS - 1, 64, FF), bf16),
            pltpu.VMEM((CHIPS - 1, 64, FF), bf16),
            dma((2,)),
            dma((5,)),
            dma((3,)),
            dma((3, PEERS)),
            dma((3, PEERS)),
            dma((PEERS,)),
            dma((PEERS,)),
            dma((4, PEERS)),
            dma((4, PEERS)),
            dma((2,)),
            dma((2,)),
            dma((4, CHIPS - 1)),
            dma((4, CHIPS - 1)),
        ],
        compiler_params=pltpu.CompilerParams(
            collective_id=0, has_side_effects=True, vmem_limit_bytes=62 * 2**20
        ),
        name="layer",
    )(
        tokens.reshape(TOK, D),
        cotangent.reshape(TOK, D),
        actions,
        action_table,
        norm_gain.reshape(1, D),
        routes.reshape(TOK, 2),
        gate_probs.reshape(TOK, 2),
        predicted.reshape(1, TOK),
        queries.reshape(TOK, D),
        key_rows.reshape(TOK, D),
        values.reshape(TOK, D),
        up_weight.reshape(D, FF),
        down_weight.reshape(FF, D),
    )
    return (
        layer_out.reshape(tokens.shape),
        stream_grad.reshape(tokens.shape),
        up_grad.reshape(1, D // PEERS, FF),
        down_grad.reshape(1, FF // PEERS, D),
    )


def solution(mesh):
    rows = P("expert", "tm", None, None)
    in_specs = (
        rows,
        rows,
        rows,
        rows,
        P("expert", "tm"),
        P(),
        P(),
        rows,
        rows,
        P("expert", "tm", None),
        rows,
        P("expert", None, None),
        P("expert", None, None),
    )
    out_specs = (rows, rows, P("expert", "tm", None), P("expert", "tm", None))
    return jax.shard_map(local, mesh=mesh, in_specs=in_specs, out_specs=out_specs, check_vma=False)
```

profile of v0, /device:TPU:1, one launch (start us, length us, event | category | flops | bytes accessed | tf_op | source)
XLA Modules:
  0.0 153.4 jit_solution(17286474788223753547)
XLA Ops:
  1.3 1.4 copy.17
  2.7 1.4 copy.18
  4.1 142.1 %layer.1 = (bf16[128,2048]{1,0:T(8,128)(2,1)}, bf16[128,2048]{1,0:T(8,128)(2,1)}, bf16[128,1024]{1,0:T(8,128)(2,1)}, bf16[64,2048]{1,0:T(8,128)(2,1)}) custom-call(bf16[128,2048]{1,0:T(8,128)(2,1)} %bitcast.17, bf16[128,2048]{1,0:T(8,128)(2,1)} %bitcast.18, s32[1,1]{1,0:T(1,128)S(6)} %copy.23.action, bf16[64,2048]{1,0:T(8,128)(2,1)} %table.1, ...), custom_call_target="tpu_custom_call" | custom-call | tf_op jit(solution)/shard_map/layer/pallas_call | solution.py:560
  146.3 1.9 %copy.24 = bf16[1,1,128,2048]{3,2,1,0:T(8,128)(2,1)} copy(bf16[1,1,128,2048]{3,2,1,0:T(8,128)(2,1)} %bitcast.23) | data formatting | bytes 1048576
  148.1 1.9 %copy.25 = bf16[1,1,128,2048]{3,2,1,0:T(8,128)(2,1)} copy(bf16[1,1,128,2048]{3,2,1,0:T(8,128)(2,1)} %bitcast.22) | data formatting | bytes 1048576
  150.0 1.7 %copy.26 = bf16[1,128,1024]{2,1,0:T(8,128)(2,1)} copy(bf16[1,128,1024]{2,1,0:T(8,128)(2,1)} %bitcast.27) | data formatting | bytes 524288
  151.7 1.7 %copy.27 = bf16[1,64,2048]{2,1,0:T(8,128)(2,1)} copy(bf16[1,64,2048]{2,1,0:T(8,128)(2,1)} %bitcast.26) | data formatting | bytes 524288
where the time goes:
time: 155 us; the launch traced here: 153 us
  Pallas kernels  142 us (92%)
  local copies, waits for them, and re-layouts  9.93 us (6%)
    pallas_call x1, Pallas kernels, local(): pl.pallas_call(layer_kernel, out_shape=(jax.ShapeDtypeStruct((TOK, D), bf...  142 us
    unnamed x6, local copies, waits for them, and re-layouts  9.93 us

commit v1 on v0

--- a/solution.py
+++ b/solution.py
@@ -55,6 +55,9 @@
     return lax.rem(y + o // 4, 4) * 4 + lax.rem(x + lax.rem(o, 4), 4)
 
 
+FAR_FIRST = (10, 2, 8, 6, 14, 9, 11, 5, 7, 13, 15, 1, 3, 4, 12)
+
+
 def far_first(s):
     half = s // 2
     return 8 + half - 2 * half * lax.rem(s, 2)
@@ -90,7 +93,8 @@
             src.at[rows_of(p), :], dst.at[rows_of(me), :], send.at[p], recv.at[me], "expert", p
         ).start()
 
-    each(1, PEERS, go)
+    for o in FAR_FIRST:
+        go(o)
     pltpu.make_async_copy(src.at[rows_of(me), :], dst.at[rows_of(me), :], own).start()
 
 
@@ -145,15 +149,19 @@
     dst[ROWS:PADDED, :] = jnp.zeros((PADDED - ROWS, D), bf16)
 
 
+def turned_row(ref, k):
+    return jnp.transpose(jnp.broadcast_to(ref[k : k + 1, :].astype(f32), (TOK, TOK)))
+
+
 def route_hots(routes, body_t, rest_t, body_k, rest_k):
     lane, row = iota((TOK, TOK), 1), iota((TOK, TOK), 0)
-    r = routes[...]
-    hit = [lane == r[:, k : k + 1] for k in range(2)]
+    r = [turned_row(routes, k) for k in range(2)]
+    hit = [lane.astype(f32) == r[k] for k in range(2)]
     hits = one_hot(jnp.logical_or(hit[0], hit[1]))
     rank = dot(one_hot(lane < row), hits)
     for k in range(2):
         mine = jnp.sum(jnp.where(hit[k], rank, 0.0), axis=1, keepdims=True)
-        base = r[:, k : k + 1].astype(f32) * BODY + mine
+        base = r[k][:, 0:1] * BODY + mine
         at_body = jnp.where(mine < BODY, base, -1.0)
         at_rest = jnp.where(mine < BODY, -1000.0, base - BODY)
         wide_body = jnp.broadcast_to(at_body, (TOK, TOK))
@@ -192,6 +200,23 @@
 
 
 def layer_kernel(
+    tok_any,
+    cot_any,
+    action_any,
+    table_any,
+    gain_any,
+    routes_any,
+    gates_any,
+    predicted_any,
+    q_any,
+    k_any,
+    v_any,
+    up_any,
+    down_any,
+    layer_any,
+    stream_grad_any,
+    up_grad_any,
+    down_grad_any,
     tok,
     cot,
     action,
@@ -200,11 +225,6 @@
     routes,
     gates,
     predicted,
-    q_any,
-    k_any,
-    v_any,
-    up_any,
-    down_any,
     layer_out,
     stream_grad,
     up_grad,
@@ -246,6 +266,8 @@
     down_left,
     up_right,
     up_left,
+    fetch_sem,
+    result_sem,
     w_sem,
     own_sem,
     qkv_own,
@@ -265,10 +287,23 @@
     sibling = tm + 1 - 2 * core
     right, left = lax.rem(tm + 2, PEERS), lax.rem(tm + PEERS - 2, PEERS)
 
+    def fetch(n, src, dst):
+        return pltpu.make_async_copy(src, dst, fetch_sem.at[n])
+
+    first = [
+        fetch(0, routes_any, routes),
+        fetch(1, gates_any, gates),
+        fetch(2, predicted_any, predicted),
+        fetch(3, cot_any, cot),
+    ]
+    later = [
+        fetch(4, tok_any, tok),
+        fetch(5, action_any, action),
+        fetch(6, table_any, table),
+        fetch(7, gain_any, gain),
+    ]
     up_load = pltpu.make_async_copy(up_any, up_w, w_sem.at[0])
     down_load = pltpu.make_async_copy(down_any, down_w, w_sem.at[1])
-    up_load.start()
-    down_load.start()
 
     def columns(p):
         return pl.ds(pl.multiple_of(p * HD, HD), HD)
@@ -278,8 +313,6 @@
         pltpu.make_async_copy(a.at[:, columns(tm)], b.at[tm], qkv_own.at[n])
         for n, (a, b) in enumerate(trio)
     ]
-    for copy in own_heads:
-        copy.start()
 
     barrier = pltpu.get_barrier_semaphore()
 
@@ -292,46 +325,51 @@
         )
 
     each(1, PEERS, greet)
-    pl.semaphore_wait(barrier, 2 * (PEERS - 1))
-
-    def send_heads(s):
-        p = tm_peer(tm, far_first(s))
-        for n, (a, b) in enumerate(trio):
-            remote(
-                a.at[:, columns(p)], b.at[tm], qkv_send.at[n, p], qkv_recv.at[n, tm], "tm", p
-            ).start()
-
-    each(1, PEERS, send_heads)
-
+    for copy in first + own_heads + later + [down_load, up_load]:
+        copy.start()
+
+    for copy in first:
+        copy.wait()
     route_hots(routes, body_t, rest_t, body_k, rest_k)
-    kept = jnp.transpose(jnp.broadcast_to(predicted[...].astype(f32), (TOK, TOK)))[:, 0:1]
+    kept = turned_row(predicted, 0)[:, 0:1]
+    gate = [turned_row(gates, k)[:, 0:1] for k in range(2)]
     upstream = cot[...].astype(f32) * kept
     for k in range(2):
-        rows[k * TOK : (k + 1) * TOK, :] = (gates[:, k : k + 1] * upstream).astype(bf16)
+        rows[k * TOK : (k + 1) * TOK, :] = (gate[k] * upstream).astype(bf16)
     pack(grad_send, body_t, rest_t, rows)
+
+    pl.semaphore_wait(barrier, 2 * (PEERS - 1))
+
+    def send_head(n, s):
+        p = tm_peer(tm, far_first(s))
+        a, b = trio[n]
+        remote(
+            a.at[:, columns(p)], b.at[tm], qkv_send.at[n, p], qkv_recv.at[n, tm], "tm", p
+        ).start()
+
+    def send_keys(s):
+        send_head(1, s)
+        send_head(2, s)
+
+    each(1, PEERS, send_keys)
     exchange_start(grad_send, grad_in, x_send.at[0], x_recv.at[0], own_sem.at[0], ex)
-
-    down_load.wait()
-    exchange_wait(grad_in, grad_in, x_send.at[0], x_recv.at[0], own_sem.at[0], ex)
-    unpack(gs, grad_in)
-
-    def act_back(n):
-        f = pl.ds(pl.multiple_of(n * 256, 256), 256)
-        grad_act[:, f] = dot_nt(gs[0:ROWS, :], down_w[f, :])
-
-    each(0, FF // 256, act_back)
+    each(1, PEERS, functools.partial(send_head, 0))
 
     for copy in own_heads:
         copy.wait()
 
-    def wait_heads(o):
+    def wait_head(n, p):
+        a, b = trio[n]
+        remote(
+            a.at[:, columns(p)], b.at[p], qkv_send.at[n, p], qkv_recv.at[n, p], "tm", p
+        ).wait_recv()
+
+    def wait_keys(o):
         p = tm_peer(tm, o)
-        for n, (a, b) in enumerate(trio):
-            remote(
-                a.at[:, columns(p)], b.at[p], qkv_send.at[n, p], qkv_recv.at[n, p], "tm", p
-            ).wait_recv()
-
-    each(1, PEERS, wait_heads)
+        wait_head(1, p)
+        wait_head(2, p)
+
+    each(1, PEERS, wait_keys)
 
     def send_attended(p):
         remote(
@@ -341,6 +379,13 @@
     def attend(s):
         half = (s + 1) // 2
         i = lax.rem(chip + 4 + half - 2 * half * lax.rem(s, 2), CHIPS)
+        for c in range(2):
+            p = 2 * i + c
+
+            @pl.when(p != tm)
+            def _():
+                wait_head(0, p)
+
         lax.switch(
             i,
             [functools.partial(attend_pair, n, qs, ks, vs, heads_out) for n in range(CHIPS)],
@@ -357,6 +402,8 @@
         heads_out.at[tm], attended.at[:, columns(tm)], own_sem.at[4]
     )
     own_out.start()
+    for copy in later:
+        copy.wait()
     choose = one_hot(iota((8, ACTIONS), 1) == jnp.broadcast_to(action[...], (8, ACTIONS)))
     action_row = dot(choose, table[...])[0:1, :]
     own_out.wait()
@@ -378,6 +425,16 @@
     rows[TOK : 2 * TOK, :] = normed
     pack(norm_send, body_t, rest_t, rows)
     exchange_start(norm_send, norm_in, x_send.at[1], x_recv.at[1], own_sem.at[1], ex)
+
+    down_load.wait()
+    exchange_wait(grad_send, grad_in, x_send.at[0], x_recv.at[0], own_sem.at[0], ex)
+    unpack(gs, grad_in)
+
+    def act_back(n):
+        f = pl.ds(pl.multiple_of(n * 256, 256), 256)
+        grad_act[:, f] = dot_nt(gs[0:ROWS, :], down_w[f, :])
+
+    each(0, FF // 256, act_back)
     up_load.wait()
     exchange_wait(norm_send, norm_in, x_send.at[1], x_recv.at[1], own_sem.at[1], ex)
     unpack(xs, norm_in)
@@ -429,11 +486,6 @@
             rest = more if rest is None else rest + more
         dst[:, D:BLOCK] = rest.astype(bf16)
 
-    send_rows(
-        out_send, lambda q: dot(act[0:ROWS, :], down_w[:, q * QUARTER : (q + 1) * QUARTER])
-    )
-    exchange_start(out_send, out_in, x_send.at[2], x_recv.at[2], own_sem.at[2], ex)
-
     streams = (
         (down_pair, down_part, down_right, 0, 32, 1, right),
         (down_pair, down_part, down_left, 32, 32, -1, left),
@@ -457,26 +509,41 @@
         pair[t, lo : lo + size, :] = chip_sum(n, t).astype(bf16)
         hop(n, pair.at[t, lo : lo + size, :], 0).start()
 
+    def next_hop(n, s):
+        _, _, slots, _, _, way, _ = streams[n]
+        t = lax.rem(chip - way * (1 + s) + 2 * CHIPS, CHIPS)
+        hop(n, slots.at[s - 1], s - 1).wait_recv()
+        slots[s - 1] = (slots[s - 1].astype(f32) + chip_sum(n, t)).astype(bf16)
+        hop(n, slots.at[s - 1], s).start()
+
     pair_down.wait_recv()
     first_hop(0)
     first_hop(1)
+    send_rows(
+        out_send, lambda q: dot(act[0:ROWS, :], down_w[:, q * QUARTER : (q + 1) * QUARTER])
+    )
+    exchange_start(out_send, out_in, x_send.at[2], x_recv.at[2], own_sem.at[2], ex)
+
     pair_up.wait_recv()
     first_hop(2)
     first_hop(3)
+    next_hop(0, 1)
+    next_hop(1, 1)
 
     send_rows(
         back_send, lambda q: dot_nt(grad_pre[0:ROWS, :], up_w[q * QUARTER : (q + 1) * QUARTER, :])
     )
     exchange_start(back_send, back_in, x_send.at[3], x_recv.at[3], own_sem.at[3], ex)
 
-    def next_hop(s):
-        for n, (_, _, slots, _, _, way, _) in enumerate(streams):
-            t = lax.rem(chip - way * (1 + s) + 2 * CHIPS, CHIPS)
-            hop(n, slots.at[s - 1], s - 1).wait_recv()
-            slots[s - 1] = (slots[s - 1].astype(f32) + chip_sum(n, t)).astype(bf16)
-            hop(n, slots.at[s - 1], s).start()
-
-    each(1, CHIPS - 1, next_hop)
+    def hops(s):
+        next_hop(2, s)
+        next_hop(3, s)
+        next_hop(0, s + 1)
+        next_hop(1, s + 1)
+
+    each(1, CHIPS - 2, hops)
+    next_hop(2, CHIPS - 2)
+    next_hop(3, CHIPS - 2)
 
     exchange_wait(out_send, out_in, x_send.at[2], x_recv.at[2], own_sem.at[2], ex)
     for q in range(4):
@@ -484,8 +551,10 @@
         mixed = stream[:, d].astype(f32)
         for k in range(2):
             picked = dot(body_k[k], out_in[:, d]) + dot(rest_k[k, q], out_in[:, D:BLOCK])
-            mixed = mixed + gates[:, k : k + 1] * picked
+            mixed = mixed + gate[k] * picked
         layer_out[:, d] = mixed.astype(bf16)
+    layer_store = pltpu.make_async_copy(layer_out, layer_any, result_sem.at[0])
+    layer_store.start()
 
     exchange_wait(back_send, back_in, x_send.at[3], x_recv.at[3], own_sem.at[3], ex)
     held = stream[...].astype(f32)
@@ -507,10 +576,8 @@
         up_here = cot[:, d].astype(f32) * kept
         stream_grad[:, d] = (up_here + inv_rms * (scaled_back[:, d] - unit * both)).astype(bf16)
 
-    for n, out in ((0, down_grad), (1, down_grad), (2, up_grad), (3, up_grad)):
-        _, _, slots, lo, size, _, _ = streams[n]
-        hop(n, slots.at[CHIPS - 2], CHIPS - 2).wait_recv()
-        out[lo : lo + size, :] = (slots[CHIPS - 2].astype(f32) + chip_sum(n, chip)).astype(bf16)
+    stream_store = pltpu.make_async_copy(stream_grad, stream_grad_any, result_sem.at[1])
+    stream_store.start()
 
     def sent(o):
         p = tm_peer(tm, o)
@@ -527,6 +594,15 @@
         ((grad_send, grad_in), (norm_send, norm_in), (out_send, out_in), (back_send, back_in))
     ):
         exchange_sent(a, b, x_send.at[n], x_recv.at[n], ex)
+    for n, out in ((0, down_grad), (1, down_grad), (2, up_grad), (3, up_grad)):
+        _, _, slots, lo, size, _, _ = streams[n]
+        hop(n, slots.at[CHIPS - 2], CHIPS - 2).wait_recv()
+        out[lo : lo + size, :] = (slots[CHIPS - 2].astype(f32) + chip_sum(n, chip)).astype(bf16)
+
+    up_store = pltpu.make_async_copy(up_grad, up_grad_any, result_sem.at[2])
+    down_store = pltpu.make_async_copy(down_grad, down_grad_any, result_sem.at[3])
+    up_store.start()
+    down_store.start()
     pair_down.wait_send()
     pair_up.wait_send()
 
@@ -535,6 +611,21 @@
             hop(n, slots.at[s], s).wait_send()
 
     each(0, CHIPS - 1, hops_sent)
+    for copy in (layer_store, stream_store, up_store, down_store):
+        copy.wait()
+
+
+def deliver_kernel(*refs):
+    made, given, held, came, left = refs[0:4], refs[4:8], refs[8:12], refs[12], refs[13]
+    inward = [pltpu.make_async_copy(made[n], held[n], came.at[n]) for n in range(4)]
+    outward = [pltpu.make_async_copy(held[n], given[n], left.at[n]) for n in range(4)]
+    for copy in inward:
+        copy.start()
+    for n in range(4):
+        inward[n].wait()
+        outward[n].start()
+    for copy in outward:
+        copy.wait()
 
 
 def local(
@@ -552,22 +643,34 @@
     up_weight,
     down_weight,
 ):
-    vmem = pl.BlockSpec(memory_space=pltpu.VMEM)
     hbm = pl.BlockSpec(memory_space=pl.ANY)
     dma = pltpu.SemaphoreType.DMA
     block = pltpu.VMEM((256, BLOCK), bf16)
     head = pltpu.VMEM((PEERS, TOK, HD), bf16)
-    layer_out, stream_grad, up_grad, down_grad = pl.pallas_call(
+    results = (
+        jax.ShapeDtypeStruct((TOK, D), bf16),
+        jax.ShapeDtypeStruct((TOK, D), bf16),
+        jax.ShapeDtypeStruct((D // PEERS, FF), bf16),
+        jax.ShapeDtypeStruct((FF // PEERS, D), bf16),
+    )
+    made = pl.pallas_call(
         layer_kernel,
-        out_shape=(
-            jax.ShapeDtypeStruct((TOK, D), bf16),
-            jax.ShapeDtypeStruct((TOK, D), bf16),
-            jax.ShapeDtypeStruct((D // PEERS, FF), bf16),
-            jax.ShapeDtypeStruct((FF // PEERS, D), bf16),
-        ),
-        in_specs=[vmem] * 8 + [hbm] * 5,
-        out_specs=(vmem,) * 4,
+        out_shape=results,
+        in_specs=[hbm] * 13,
+        out_specs=(hbm,) * 4,
         scratch_shapes=[
+            pltpu.VMEM((TOK, D), bf16),
+            pltpu.VMEM((TOK, D), bf16),
+            pltpu.VMEM((1, 1), jnp.int32),
+            pltpu.VMEM((ACTIONS, D), bf16),
+            pltpu.VMEM((1, D), f32),
+            pltpu.VMEM((2, TOK), jnp.int32),
+            pltpu.VMEM((2, TOK), f32),
+            pltpu.VMEM((1, TOK), jnp.int32),
+            pltpu.VMEM((TOK, D), bf16),
+            pltpu.VMEM((TOK, D), bf16),
+            pltpu.VMEM((D // PEERS, FF), bf16),
+            pltpu.VMEM((FF // PEERS, D), bf16),
             pltpu.VMEM((D, FF), bf16),
             pltpu.VMEM((FF, D), bf16),
             head,
@@ -600,6 +703,8 @@
             pltpu.VMEM((CHIPS - 1, 32, D), bf16),
             pltpu.VMEM((CHIPS - 1, 64, FF), bf16),
             pltpu.VMEM((CHIPS - 1, 64, FF), bf16),
+            dma((8,)),
+            dma((4,)),
             dma((2,)),
             dma((5,)),
             dma((3,)),
@@ -624,8 +729,8 @@
         actions,
         action_table,
         norm_gain.reshape(1, D),
-        routes.reshape(TOK, 2),
-        gate_probs.reshape(TOK, 2),
+        routes.reshape(TOK, 2).T,
+        gate_probs.reshape(TOK, 2).T,
         predicted.reshape(1, TOK),
         queries.reshape(TOK, D),
         key_rows.reshape(TOK, D),
@@ -633,6 +738,14 @@
         up_weight.reshape(D, FF),
         down_weight.reshape(FF, D),
     )
+    layer_out, stream_grad, up_grad, down_grad = pl.pallas_call(
+        deliver_kernel,
+        out_shape=results,
+        in_specs=[hbm] * 4,
+        out_specs=(hbm,) * 4,
+        scratch_shapes=[pltpu.VMEM(r.shape, r.dtype) for r in results] + [dma((4,)), dma((4,))],
+        name="deliver",
+    )(*made)
     return (
         layer_out.reshape(tokens.shape),
         stream_grad.reshape(tokens.shape),

time: 155 us -> 137 us (0.88); the launches traced: 153 us -> 137 us
  local copies, waits for them, and re-layouts: 9.93 us -> 0 us
  Pallas kernels: 142 us -> 136 us
    unnamed x6 -> x0, local copies, waits for them, and re-layouts: 9.93 us -> none
    pallas_call x1 -> x2, Pallas kernels: 142 us -> 136 us  [the longest x1 133 us: local(): pl.pallas_call(layer_kernel, out_shape=results, in_specs=[hbm] * 13, out_...]
where the time goes in v1:
time: 137 us
  Pallas kernels  136 us (99%)
  between operations  1.45 us (1%)
    pallas_call x1, Pallas kernels, local(): pl.pallas_call(layer_kernel, out_shape=results, in_specs=[hbm] * 13, out_...  133 us

profile of v1, /device:TPU:1, one launch (start us, length us, event | category | flops | bytes accessed | tf_op | source)
XLA Modules:
  0.0 137.1 jit_solution(16005815883767137818)
XLA Ops:
  1.3 133.4 %layer.1 = (bf16[128,2048]{1,0:T(8,128)(2,1)}, bf16[128,2048]{1,0:T(8,128)(2,1)}, bf16[128,1024]{1,0:T(8,128)(2,1)}, bf16[64,2048]{1,0:T(8,128)(2,1)}) custom-call(bf16[128,2048]{1,0:T(8,128)(2,1)} %bitcast.21, bf16[128,2048]{1,0:T(8,128)(2,1)} %bitcast.22, s32[1,1]{1,0:T(1,128)S(6)} %copy.17.action_any, bf16[64,2048]{1,0:T(8,128)(2,1)} %table_any.1, ...), custom_call_target="tpu_custom_call" | custom-call | tf_op jit(solution)/shard_map/layer/pallas_call | solution.py:656
  134.7 2.2 %deliver.1 = (bf16[128,2048]{1,0:T(8,128)(2,1)}, bf16[128,2048]{1,0:T(8,128)(2,1)}, bf16[128,1024]{1,0:T(8,128)(2,1)}, bf16[64,2048]{1,0:T(8,128)(2,1)}) custom-call(bf16[128,2048]{1,0:T(8,128)(2,1)} %get-tuple-element.12.refs_0_, bf16[128,2048]{1,0:T(8,128)(2,1)} %get-tuple-element.13.refs_1_, bf16[128,1024]{1,0:T(8,128)(2,1)} %get-tuple-element.14.refs_2_, ...), custom_call_target="tpu_custom_call" | custom-call | tf_op jit(solution)/shard_map/deliver/pallas_call | solution.py:741

commit v2 on v1

--- a/solution.py
+++ b/solution.py
@@ -22,6 +22,10 @@
 PADDED = 384
 QUARTER = 512
 BLOCK = D + QUARTER
+HALF = D // 2
+PIECE = HALF // 4
+HALF_BLOCK = HALF + PIECE
+PHASES = 2
 
 norm_eps = 1e-06
 gelu_coef = 0.7978845608028654
@@ -130,6 +134,17 @@
     dst[:, D:BLOCK] = rest.astype(bf16)
 
 
+def pack_half(dst, body_hot, rest_hot, src):
+    for q in range(2):
+        d = slice(q * QUARTER, (q + 1) * QUARTER)
+        dst[:, d] = dot(body_hot[...], src[:, d]).astype(bf16)
+    rest = None
+    for q in range(4):
+        more = dot(rest_hot[q], src[:, q * PIECE : (q + 1) * PIECE])
+        rest = more if rest is None else rest + more
+    dst[:, HALF:HALF_BLOCK] = rest.astype(bf16)
+
+
 def rest_pick(q):
     i, j = iota((64, 256), 0), iota((64, 256), 1)
     return one_hot(j == (i // REST) * BODY + q * REST + lax.rem(i, REST))
@@ -151,6 +166,22 @@
 
 def turned_row(ref, k):
     return jnp.transpose(jnp.broadcast_to(ref[k : k + 1, :].astype(f32), (TOK, TOK)))
+
+
+def unpack_half(dst, src, phase):
+    lo = phase * HALF
+    dst[0:256, lo : lo + HALF] = src[:, 0:HALF]
+    for q in range(4):
+        at = lo + q * PIECE
+        dst[256:ROWS, at : at + PIECE] = dot(rest_pick(q), src[:, HALF:HALF_BLOCK]).astype(bf16)
+    dst[ROWS:PADDED, lo : lo + HALF] = jnp.zeros((PADDED - ROWS, HALF), bf16)
+
+
+def three_parts(v):
+    high = v.astype(bf16)
+    low = v - high.astype(f32)
+    middle = low.astype(bf16)
+    return high.astype(f32), middle.astype(f32), low - middle.astype(f32)
 
 
 def route_hots(routes, body_t, rest_t, body_k, rest_k):
@@ -179,24 +210,23 @@
                 rest_t[q, rows, k * TOK : (k + 1) * TOK] = one_hot(here == turned_rest + REST * q)
 
 
-def attend_pair(i, qs, ks, vs, out):
+def attend_frame(i, core, qs, ks, vs, out):
     scale = HD**-0.5
-    q = qs[2 * i : 2 * i + 2].reshape(2 * TOK, HD)
-    near = dot_nt(q, ks[2 * i : 2 * i + 2].reshape(2 * TOK, HD))
-    seen = iota((2 * TOK, 2 * TOK), 1) // TOK <= iota((2 * TOK, 2 * TOK), 0) // TOK
-    near = jnp.where(seen, near, -1e30)
+    q = qs[i]
+    near = dot_nt(q, ks[i].reshape(2 * TOK, HD))
+    near = jnp.where(iota((TOK, 2 * TOK), 1) // TOK <= core, near, -1e30)
     top = jnp.max(near, axis=1, keepdims=True)
     if i:
-        far = dot_nt(q, ks[0 : 2 * i].reshape(2 * i * TOK, HD))
+        far = dot_nt(q, ks[0:i].reshape(2 * i * TOK, HD))
         top = jnp.maximum(top, jnp.max(far, axis=1, keepdims=True))
     near = jnp.exp((near - top) * scale)
     total = jnp.sum(near, axis=1, keepdims=True)
-    acc = dot(near.astype(bf16), vs[2 * i : 2 * i + 2].reshape(2 * TOK, HD))
+    acc = dot(near.astype(bf16), vs[i].reshape(2 * TOK, HD))
     if i:
         far = jnp.exp((far - top) * scale)
         total = total + jnp.sum(far, axis=1, keepdims=True)
-        acc = acc + dot(far.astype(bf16), vs[0 : 2 * i].reshape(2 * i * TOK, HD))
-    out[2 * i : 2 * i + 2] = (acc / total).astype(bf16).reshape(2, TOK, HD)
+        acc = acc + dot(far.astype(bf16), vs[0:i].reshape(2 * i * TOK, HD))
+    out[i] = (acc / total).astype(bf16)
 
 
 def layer_kernel(
@@ -244,8 +274,13 @@
     rest_k,
     grad_send,
     grad_in,
-    norm_send,
-    norm_in,
+    first_send,
+    first_in,
+    second_send,
+    second_in,
+    squares,
+    inv_slots,
+    pre,
     out_send,
     out_in,
     back_send,
@@ -257,6 +292,7 @@
     act_t,
     grad_act,
     grad_pre,
+    grad_norm,
     scaled_back,
     down_part,
     up_part,
@@ -273,6 +309,9 @@
     qkv_own,
     qkv_send,
     qkv_recv,
+    hand_send,
+    hand_recv,
+    o_own,
     o_send,
     o_recv,
     x_send,
@@ -308,10 +347,34 @@
     def columns(p):
         return pl.ds(pl.multiple_of(p * HD, HD), HD)
 
-    trio = ((q_any, qs), (k_any, ks), (v_any, vs))
+    def head_of(phase, t):
+        return columns(phase * CHIPS + t)
+
+    def device_of(t):
+        return 2 * t + core
+
+    def other_chip(o):
+        return lax.rem(chip + o, CHIPS)
+
+    def far_chip(s):
+        half = s // 2
+        return other_chip(4 + half - 2 * half * lax.rem(s, 2))
+
+    def head_copy(n, phase, t, slot):
+        src = (q_any, k_any, v_any)[n].at[:, head_of(phase, t)]
+        dst = qs.at[phase, slot] if n == 0 else (ks, vs)[n - 1].at[phase, slot, core]
+        return src, dst
+
+    def head_remote(n, phase, t, slot):
+        src, dst = head_copy(n, phase, t, slot)
+        return remote(
+            src, dst, qkv_send.at[phase, n, t], qkv_recv.at[phase, n, slot], "tm", device_of(t)
+        )
+
     own_heads = [
-        pltpu.make_async_copy(a.at[:, columns(tm)], b.at[tm], qkv_own.at[n])
-        for n, (a, b) in enumerate(trio)
+        pltpu.make_async_copy(*head_copy(n, phase, chip, chip), qkv_own.at[phase, n])
+        for phase in range(PHASES)
+        for n in range(3)
     ]
 
     barrier = pltpu.get_barrier_semaphore()
@@ -340,142 +403,238 @@
 
     pl.semaphore_wait(barrier, 2 * (PEERS - 1))
 
-    def send_head(n, s):
-        p = tm_peer(tm, far_first(s))
-        a, b = trio[n]
-        remote(
-            a.at[:, columns(p)], b.at[tm], qkv_send.at[n, p], qkv_recv.at[n, tm], "tm", p
-        ).start()
-
-    def send_keys(s):
-        send_head(1, s)
-        send_head(2, s)
-
-    each(1, PEERS, send_keys)
+    def send_keys(phase):
+        def go(s):
+            t = far_chip(s)
+            head_remote(1, phase, t, chip).start()
+            head_remote(2, phase, t, chip).start()
+
+        each(1, CHIPS, go)
+
+    def send_queries(phase):
+        each(1, CHIPS, lambda s: head_remote(0, phase, far_chip(s), chip).start())
+
+    send_keys(0)
+    send_queries(0)
     exchange_start(grad_send, grad_in, x_send.at[0], x_recv.at[0], own_sem.at[0], ex)
-    each(1, PEERS, functools.partial(send_head, 0))
+    send_keys(1)
 
     for copy in own_heads:
         copy.wait()
 
-    def wait_head(n, p):
-        a, b = trio[n]
-        remote(
-            a.at[:, columns(p)], b.at[p], qkv_send.at[n, p], qkv_recv.at[n, p], "tm", p
-        ).wait_recv()
-
-    def wait_keys(o):
-        p = tm_peer(tm, o)
-        wait_head(1, p)
-        wait_head(2, p)
-
-    each(1, PEERS, wait_keys)
-
-    def send_attended(p):
-        remote(
-            heads_out.at[p], attended.at[:, columns(tm)], o_send.at[p], o_recv.at[tm], "tm", p
-        ).start()
-
-    def attend(s):
-        half = (s + 1) // 2
-        i = lax.rem(chip + 4 + half - 2 * half * lax.rem(s, 2), CHIPS)
-        for c in range(2):
-            p = 2 * i + c
-
-            @pl.when(p != tm)
+    def hand(phase, n, which):
+        ref = (ks, vs)[n].at[phase, :, which]
+        return remote(ref, ref, hand_send.at[phase, n], hand_recv.at[phase, n], "tm", sibling)
+
+    def wait_keys(phase):
+        def go(o):
+            t = other_chip(o)
+            head_remote(1, phase, t, t).wait_recv()
+            head_remote(2, phase, t, t).wait_recv()
+
+        each(1, CHIPS, go)
+        for n in range(2):
+            hand(phase, n, core).start()
+
+    def wait_handed(phase):
+        for n in range(2):
+            hand(phase, n, 1 - core).wait_recv()
+
+    def head_out(phase, t, slot):
+        return remote(
+            heads_out.at[phase, t],
+            attended.at[:, head_of(phase, slot)],
+            o_send.at[phase, t],
+            o_recv.at[phase, slot],
+            "tm",
+            device_of(t),
+        )
+
+    def own_out(phase):
+        return pltpu.make_async_copy(
+            heads_out.at[phase, chip], attended.at[:, head_of(phase, chip)], o_own.at[phase]
+        )
+
+    def attend(phase):
+        def go(s):
+            half = (s + 1) // 2
+            i = lax.rem(chip + 4 + half - 2 * half * lax.rem(s, 2), CHIPS)
+
+            @pl.when(i != chip)
             def _():
-                wait_head(0, p)
-
-        lax.switch(
-            i,
-            [functools.partial(attend_pair, n, qs, ks, vs, heads_out) for n in range(CHIPS)],
-        )
-        for c in range(2):
-            p = 2 * i + c
-
-            @pl.when(p != tm)
+                head_remote(0, phase, i, i).wait_recv()
+
+            lax.switch(
+                i,
+                [
+                    functools.partial(
+                        attend_frame,
+                        n,
+                        core,
+                        qs.at[phase],
+                        ks.at[phase],
+                        vs.at[phase],
+                        heads_out.at[phase],
+                    )
+                    for n in range(CHIPS)
+                ],
+            )
+
+            @pl.when(i != chip)
             def _():
-                send_attended(p)
-
-    each(0, CHIPS, attend)
-    own_out = pltpu.make_async_copy(
-        heads_out.at[tm], attended.at[:, columns(tm)], own_sem.at[4]
-    )
-    own_out.start()
+                head_out(phase, i, chip).start()
+
+        each(0, CHIPS, go)
+        own_out(phase).start()
+
+    def wait_attended(phase):
+        own_out(phase).wait()
+
+        def go(o):
+            t = other_chip(o)
+            head_out(phase, t, t).wait_recv()
+
+        each(1, CHIPS, go)
+
+    def columns_done(phase):
+        d = slice(phase * HALF, (phase + 1) * HALF)
+        total = tok[:, d].astype(f32) + attended[:, d].astype(f32) + action_row[:, d]
+        stream[:, d] = total.astype(bf16)
+        held = stream[:, d].astype(f32)
+        part = (held * gain[:, d]).astype(bf16)
+        rows[0:TOK, 0:HALF] = part
+        rows[TOK : 2 * TOK, 0:HALF] = part
+        return jnp.sum(held * held, axis=1, keepdims=True)
+
+    def turn(phase):
+        for n in range(4):
+            lo = phase * HALF + n * 256
+            turned[phase * 4 + n] = jnp.transpose(xs[:, lo : lo + 256]).reshape(2, 128, PADDED)
+
+    wait_keys(0)
+    wait_handed(0)
+    attend(0)
+    send_queries(1)
+
+    down_load.wait()
+    exchange_wait(grad_send, grad_in, x_send.at[0], x_recv.at[0], own_sem.at[0], ex)
+    unpack(gs, grad_in)
+
+    def act_back(n):
+        f = pl.ds(pl.multiple_of(n * 256, 256), 256)
+        grad_act[:, f] = dot_nt(gs[0:ROWS, :], down_w[f, :])
+
+    each(0, FF // 256, act_back)
     for copy in later:
         copy.wait()
     choose = one_hot(iota((8, ACTIONS), 1) == jnp.broadcast_to(action[...], (8, ACTIONS)))
     action_row = dot(choose, table[...])[0:1, :]
-    own_out.wait()
-
-    def wait_attended(o):
-        p = tm_peer(tm, o)
-        remote(
-            heads_out.at[p], attended.at[:, columns(p)], o_send.at[p], o_recv.at[p], "tm", p
-        ).wait_recv()
-
-    each(1, PEERS, wait_attended)
-
-    total = tok[...].astype(f32) + attended[...].astype(f32) + action_row
-    stream[...] = total.astype(bf16)
-    held = stream[...].astype(f32)
-    inv_rms = lax.rsqrt(jnp.mean(held * held, axis=1, keepdims=True) + norm_eps)
-    normed = (held * inv_rms * gain[...]).astype(bf16)
-    rows[0:TOK, :] = normed
-    rows[TOK : 2 * TOK, :] = normed
-    pack(norm_send, body_t, rest_t, rows)
-    exchange_start(norm_send, norm_in, x_send.at[1], x_recv.at[1], own_sem.at[1], ex)
-
-    down_load.wait()
-    exchange_wait(grad_send, grad_in, x_send.at[0], x_recv.at[0], own_sem.at[0], ex)
-    unpack(gs, grad_in)
-
-    def act_back(n):
+
+    wait_keys(1)
+    wait_attended(0)
+    squares[...] = columns_done(0)
+    pack_half(first_send, body_t, rest_t, rows)
+    exchange_start(first_send, first_in, x_send.at[1], x_recv.at[1], own_sem.at[1], ex)
+    wait_handed(1)
+    attend(1)
+    wait_attended(1)
+
+    inv_rms = lax.rsqrt((squares[...] + columns_done(1)) * (1.0 / D) + norm_eps)
+    pack_half(second_send, body_t, rest_t, rows)
+    lane = iota((TOK, TOK), 1)
+    in_body = in_rest = jnp.zeros((TOK, TOK), f32)
+    for n, part in enumerate(three_parts(inv_rms)):
+        in_body = jnp.where(lane == n, part, in_body)
+        in_rest = jnp.where(lane == n + 3, part, in_rest)
+    in_body, in_rest = in_body.astype(bf16), in_rest.astype(bf16)
+    second_send[:, HALF_BLOCK:] = (
+        dot(body_t[:, 0:TOK] + body_t[:, TOK:], in_body)
+        + dot(rest_t[0, :, 0:TOK] + rest_t[0, :, TOK:], in_rest)
+    ).astype(bf16)
+    exchange_start(second_send, second_in, x_send.at[4], x_recv.at[4], own_sem.at[4], ex)
+
+    up_load.wait()
+    exchange_wait(first_send, first_in, x_send.at[1], x_recv.at[1], own_sem.at[1], ex)
+    unpack_half(xs, first_in, 0)
+
+    def first_up(n):
         f = pl.ds(pl.multiple_of(n * 256, 256), 256)
-        grad_act[:, f] = dot_nt(gs[0:ROWS, :], down_w[f, :])
-
-    each(0, FF // 256, act_back)
-    up_load.wait()
-    exchange_wait(norm_send, norm_in, x_send.at[1], x_recv.at[1], own_sem.at[1], ex)
-    unpack(xs, norm_in)
+        pre[:, f] = dot(xs[0:ROWS, 0:HALF], up_w[0:HALF, f])
+
+    each(0, FF // 256, first_up)
+    turn(0)
+    exchange_wait(second_send, second_in, x_send.at[4], x_recv.at[4], own_sem.at[4], ex)
+    unpack_half(xs, second_in, 1)
+    parts = second_in[:, HALF_BLOCK:]
+    lane = iota((256, TOK), 1)
+    inv_slots[0:256, :] = jnp.sum(
+        jnp.where(lane < 3, parts.astype(f32), 0.0), axis=1, keepdims=True
+    )
+    lane = iota((64, TOK), 1)
+    inv_slots[256:ROWS, :] = jnp.sum(
+        jnp.where(jnp.logical_and(lane >= 3, lane < 6), dot(rest_pick(0), parts), 0.0),
+        axis=1,
+        keepdims=True,
+    )
 
     act[ROWS:PADDED, :] = jnp.zeros((PADDED - ROWS, FF), bf16)
     grad_pre[ROWS:PADDED, :] = jnp.zeros((PADDED - ROWS, FF), bf16)
 
+    grad_norm[ROWS:PADDED, :] = jnp.zeros((PADDED - ROWS, FF), bf16)
+
     def expert_up(n):
         f = pl.ds(pl.multiple_of(n * 256, 256), 256)
-        v = dot(xs[0:ROWS, :], up_w[:, f])
+        inv = inv_slots[...]
+        v = (pre[:, f] + dot(xs[0:ROWS, HALF:D], up_w[HALF:D, f])) * inv
         th = jnp.tanh(gelu_coef * (v + 0.044715 * v * v * v))
         act[0:ROWS, f] = (0.5 * v * (1.0 + th)).astype(bf16)
         slope = 0.5 * (1.0 + th) + 0.5 * v * (1.0 - th * th) * gelu_coef * (
             1.0 + 3.0 * 0.044715 * v * v
         )
-        grad_pre[0:ROWS, f] = (grad_act[:, f] * slope).astype(bf16)
-        act_t[f, :] = jnp.transpose(act[:, f])
+        back = grad_act[:, f] * slope
+        grad_pre[0:ROWS, f] = back.astype(bf16)
+        grad_norm[0:ROWS, f] = (back * inv).astype(bf16)
+        act_t[pl.ds(n * 2, 2)] = jnp.transpose(act[:, f]).reshape(2, 2, 64, PADDED)
 
     each(0, FF // 256, expert_up)
 
-    def down_weights(n):
-        d = pl.ds(pl.multiple_of(n * 512, 512), 512)
-        down_part[:, :, :, d] = dot(act_t[...], gs[:, d]).astype(bf16).reshape(CHIPS, 2, 64, 512)
-
-    each(0, D // 512, down_weights)
-    pair_down = remote(
-        down_part.at[:, 1 - core], down_pair, pair_send.at[0], pair_recv.at[0], "tm", sibling
-    )
-    pair_down.start()
-
-    def up_weights(n):
-        d = pl.ds(pl.multiple_of(n * 512, 512), 512)
-        turned[...] = jnp.transpose(xs[:, d])
-        part = dot(turned[...], grad_pre[...]).astype(bf16)
-        up_part[pl.ds(n * 2, 2)] = part.reshape(2, 2, 128, FF)
-
-    each(0, D // 512, up_weights)
-    pair_up = remote(
-        up_part.at[:, 1 - core], up_pair, pair_send.at[1], pair_recv.at[1], "tm", sibling
-    )
-    pair_up.start()
+    def down_weights(which):
+        def go(n):
+            d = pl.ds(pl.multiple_of(n * 512, 512), 512)
+            part = dot(act_t[:, which].reshape(CHIPS * 64, PADDED), gs[:, d]).astype(bf16)
+            down_part[:, which, :, d] = part.reshape(CHIPS, 64, 512)
+
+        each(0, D // 512, go)
+
+    def up_weights(which):
+        def go(n):
+            part = dot(turned[pl.ds(n * 2, 2), which].reshape(256, PADDED), grad_norm[...])
+            up_part[pl.ds(n * 2, 2), which] = part.astype(bf16).reshape(2, 128, FF)
+
+        each(0, CHIPS // 2, go)
+
+    def pair(n, t):
+        part, got = ((down_part, down_pair), (up_part, up_pair))[n]
+        return remote(
+            part.at[t, 1 - core], got.at[t], pair_send.at[n, t], pair_recv.at[n, t], "tm", sibling
+        )
+
+    def pair_start(n):
+        for o in (7, 1, 6, 2, 5, 3, 4, 0):
+            pair(n, other_chip(o)).start()
+
+    def pair_wait(n, offsets):
+        for o in offsets:
+            pair(n, other_chip(o)).wait_recv()
+
+    near_chips, far_chips = (7, 1), (6, 2, 5, 3, 4, 0)
+
+    down_weights(1 - core)
+    pair_start(0)
+    turn(1)
+    down_weights(core)
+    up_weights(1 - core)
+    pair_start(1)
 
     def send_rows(dst, product):
         rest = None
@@ -516,17 +675,20 @@
         slots[s - 1] = (slots[s - 1].astype(f32) + chip_sum(n, t)).astype(bf16)
         hop(n, slots.at[s - 1], s).start()
 
-    pair_down.wait_recv()
+    pair_wait(0, near_chips)
     first_hop(0)
     first_hop(1)
+    up_weights(core)
+    pair_wait(1, near_chips)
+    first_hop(2)
+    first_hop(3)
     send_rows(
         out_send, lambda q: dot(act[0:ROWS, :], down_w[:, q * QUARTER : (q + 1) * QUARTER])
     )
     exchange_start(out_send, out_in, x_send.at[2], x_recv.at[2], own_sem.at[2], ex)
 
-    pair_up.wait_recv()
-    first_hop(2)
-    first_hop(3)
+    pair_wait(0, far_chips)
+    pair_wait(1, far_chips)
     next_hop(0, 1)
     next_hop(1, 1)
 
@@ -580,20 +742,33 @@
     stream_store.start()
 
     def sent(o):
-        p = tm_peer(tm, o)
-        for n, (a, b) in enumerate(trio):
-            remote(
-                a.at[:, columns(p)], b.at[p], qkv_send.at[n, p], qkv_recv.at[n, p], "tm", p
-            ).wait_send()
-        remote(
-            heads_out.at[p], attended.at[:, columns(p)], o_send.at[p], o_recv.at[p], "tm", p
-        ).wait_send()
-
-    each(1, PEERS, sent)
+        t = other_chip(o)
+        for phase in range(PHASES):
+            for n in range(3):
+                head_remote(n, phase, t, t).wait_send()
+            head_out(phase, t, t).wait_send()
+
+    each(1, CHIPS, sent)
+    for phase in range(PHASES):
+        for n in range(2):
+            hand(phase, n, core).wait_send()
     for n, (a, b) in enumerate(
-        ((grad_send, grad_in), (norm_send, norm_in), (out_send, out_in), (back_send, back_in))
+        (
+            (grad_send, grad_in),
+            (first_send, first_in),
+            (out_send, out_in),
+            (back_send, back_in),
+            (second_send, second_in),
+        )
     ):
         exchange_sent(a, b, x_send.at[n], x_recv.at[n], ex)
+
+    def pairs_sent(t):
+        pair(0, t).wait_send()
+        pair(1, t).wait_send()
+
+    each(0, CHIPS, pairs_sent)
+
     for n, out in ((0, down_grad), (1, down_grad), (2, up_grad), (3, up_grad)):
         _, _, slots, lo, size, _, _ = streams[n]
         hop(n, slots.at[CHIPS - 2], CHIPS - 2).wait_recv()
@@ -603,8 +778,6 @@
     down_store = pltpu.make_async_copy(down_grad, down_grad_any, result_sem.at[3])
     up_store.start()
     down_store.start()
-    pair_down.wait_send()
-    pair_up.wait_send()
 
     def hops_sent(s):
         for n, (_, _, slots, _, _, _, _) in enumerate(streams):
@@ -646,7 +819,6 @@
     hbm = pl.BlockSpec(memory_space=pl.ANY)
     dma = pltpu.SemaphoreType.DMA
     block = pltpu.VMEM((256, BLOCK), bf16)
-    head = pltpu.VMEM((PEERS, TOK, HD), bf16)
     results = (
         jax.ShapeDtypeStruct((TOK, D), bf16),
         jax.ShapeDtypeStruct((TOK, D), bf16),
@@ -673,10 +845,10 @@
             pltpu.VMEM((FF // PEERS, D), bf16),
             pltpu.VMEM((D, FF), bf16),
             pltpu.VMEM((FF, D), bf16),
-            head,
-            head,
-            head,
-            head,
+            pltpu.VMEM((PHASES, CHIPS, TOK, HD), bf16),
+            pltpu.VMEM((PHASES, CHIPS, 2, TOK, HD), bf16),
+            pltpu.VMEM((PHASES, CHIPS, 2, TOK, HD), bf16),
+            pltpu.VMEM((PHASES, CHIPS, TOK, HD), bf16),
             pltpu.VMEM((TOK, D), bf16),
             pltpu.VMEM((TOK, D), bf16),
             pltpu.VMEM((2 * TOK, D), bf16),
@@ -685,14 +857,25 @@
             pltpu.VMEM((2, TOK, 256), bf16),
             pltpu.VMEM((2, 4, TOK, 256), bf16),
         ]
-        + [block] * 8
+        + [block] * 2
+        + [
+            pltpu.VMEM((256, HALF_BLOCK), bf16),
+            pltpu.VMEM((256, HALF_BLOCK), bf16),
+            pltpu.VMEM((256, HALF_BLOCK + TOK), bf16),
+            pltpu.VMEM((256, HALF_BLOCK + TOK), bf16),
+            pltpu.VMEM((TOK, 1), f32),
+            pltpu.VMEM((ROWS, 1), f32),
+            pltpu.VMEM((ROWS, FF), f32),
+        ]
+        + [block] * 4
         + [
             pltpu.VMEM((PADDED, D), bf16),
             pltpu.VMEM((PADDED, D), bf16),
-            pltpu.VMEM((512, PADDED), bf16),
+            pltpu.VMEM((CHIPS, 2, 128, PADDED), bf16),
             pltpu.VMEM((PADDED, FF), bf16),
-            pltpu.VMEM((FF, PADDED), bf16),
+            pltpu.VMEM((CHIPS, 2, 64, PADDED), bf16),
             pltpu.VMEM((ROWS, FF), f32),
+            pltpu.VMEM((PADDED, FF), bf16),
             pltpu.VMEM((PADDED, FF), bf16),
             pltpu.VMEM((TOK, D), f32),
             pltpu.VMEM((CHIPS, 2, 64, D), bf16),
@@ -707,15 +890,18 @@
             dma((4,)),
             dma((2,)),
             dma((5,)),
-            dma((3,)),
-            dma((3, PEERS)),
-            dma((3, PEERS)),
-            dma((PEERS,)),
-            dma((PEERS,)),
-            dma((4, PEERS)),
-            dma((4, PEERS)),
-            dma((2,)),
-            dma((2,)),
+            dma((PHASES, 3)),
+            dma((PHASES, 3, CHIPS)),
+            dma((PHASES, 3, CHIPS)),
+            dma((PHASES, 2)),
+            dma((PHASES, 2)),
+            dma((PHASES,)),
+            dma((PHASES, CHIPS)),
+            dma((PHASES, CHIPS)),
+            dma((5, PEERS)),
+            dma((5, PEERS)),
+            dma((2, CHIPS)),
+            dma((2, CHIPS)),
             dma((4, CHIPS - 1)),
             dma((4, CHIPS - 1)),
         ],

time: 137 us -> 126 us (0.920)
  Pallas kernels: 136 us -> 125 us
    pallas_call x1, Pallas kernels: 133 us -> 122 us  [local(): pl.pallas_call(layer_kernel, out_shape=results, in_specs=[hbm] * 13, out_...]
where the time goes in v2:
time: 126 us
  Pallas kernels  125 us (99%)
  between operations  1.45 us (1%)
    pallas_call x1, Pallas kernels, local(): pl.pallas_call(layer_kernel, out_shape=results, in_specs=[hbm] * 13, out_...  122 us

profile of v2, /device:TPU:1, one launch (start us, length us, event | category | flops | bytes accessed | tf_op | source)
XLA Modules:
  0.0 126.2 jit_solution(14875768736352030006)
XLA Ops:
  1.3 122.5 %layer.1 = (bf16[128,2048]{1,0:T(8,128)(2,1)}, bf16[128,2048]{1,0:T(8,128)(2,1)}, bf16[128,1024]{1,0:T(8,128)(2,1)}, bf16[64,2048]{1,0:T(8,128)(2,1)}) custom-call(bf16[128,2048]{1,0:T(8,128)(2,1)} %bitcast.21, bf16[128,2048]{1,0:T(8,128)(2,1)} %bitcast.22, s32[1,1]{1,0:T(1,128)S(6)} %copy.17.action_any, bf16[64,2048]{1,0:T(8,128)(2,1)} %table_any.1, ...), custom_call_target="tpu_custom_call" | custom-call | tf_op jit(solution)/shard_map/layer/pallas_call | solution.py:828
  123.8 2.2 %deliver.1 = (bf16[128,2048]{1,0:T(8,128)(2,1)}, bf16[128,2048]{1,0:T(8,128)(2,1)}, bf16[128,1024]{1,0:T(8,128)(2,1)}, bf16[64,2048]{1,0:T(8,128)(2,1)}) custom-call(bf16[128,2048]{1,0:T(8,128)(2,1)} %get-tuple-element.12.refs_0_, bf16[128,2048]{1,0:T(8,128)(2,1)} %get-tuple-element.13.refs_1_, bf16[128,1024]{1,0:T(8,128)(2,1)} %get-tuple-element.14.refs_2_, ...), custom_call_target="tpu_custom_call" | custom-call | tf_op jit(solution)/shard_map/deliver/pallas_call | solution.py:927

commit v3 on v2

--- a/solution.py
+++ b/solution.py
@@ -379,17 +379,30 @@
 
     barrier = pltpu.get_barrier_semaphore()
 
-    def greet(o):
-        pl.semaphore_signal(
-            barrier, inc=1, device_id={"tm": tm_peer(tm, o)}, device_id_type=MESH
-        )
-        pl.semaphore_signal(
-            barrier, inc=1, device_id={"expert": expert_peer(ex, o)}, device_id_type=MESH
-        )
-
-    each(1, PEERS, greet)
+    def signal(axis, peer):
+        pl.semaphore_signal(barrier, inc=1, device_id={axis: peer}, device_id_type=MESH)
+
+    signal("tm", sibling)
+    each(1, CHIPS, lambda o: signal("tm", device_of(other_chip(o))))
+    each(1, PEERS, lambda o: signal("expert", expert_peer(ex, o)))
     for copy in first + own_heads + later + [down_load, up_load]:
         copy.start()
+
+    pl.semaphore_wait(barrier, CHIPS + PEERS - 1)
+
+    def send_keys(phase):
+        def go(s):
+            t = far_chip(s)
+            head_remote(1, phase, t, chip).start()
+            head_remote(2, phase, t, chip).start()
+
+        each(1, CHIPS, go)
+
+    def send_queries(phase):
+        each(1, CHIPS, lambda s: head_remote(0, phase, far_chip(s), chip).start())
+
+    send_keys(0)
+    send_queries(0)
 
     for copy in first:
         copy.wait()
@@ -401,21 +414,6 @@
         rows[k * TOK : (k + 1) * TOK, :] = (gate[k] * upstream).astype(bf16)
     pack(grad_send, body_t, rest_t, rows)
 
-    pl.semaphore_wait(barrier, 2 * (PEERS - 1))
-
-    def send_keys(phase):
-        def go(s):
-            t = far_chip(s)
-            head_remote(1, phase, t, chip).start()
-            head_remote(2, phase, t, chip).start()
-
-        each(1, CHIPS, go)
-
-    def send_queries(phase):
-        each(1, CHIPS, lambda s: head_remote(0, phase, far_chip(s), chip).start())
-
-    send_keys(0)
-    send_queries(0)
     exchange_start(grad_send, grad_in, x_send.at[0], x_recv.at[0], own_sem.at[0], ex)
     send_keys(1)
 

time: 126 us -> 126 us (level)
  no operation moved by 1% of the time
where the time goes in v3:
time: 126 us
  Pallas kernels  124 us (98%)
  between operations  1.45 us (1%)
    pallas_call x1, Pallas kernels, local(): pl.pallas_call(layer_kernel, out_shape=results, in_specs=[hbm] * 13, out_...  122 us

profile of v3, /device:TPU:1, one launch (start us, length us, event | category | flops | bytes accessed | tf_op | source)
XLA Modules:
  0.0 125.7 jit_solution(6525480025537729159)
XLA Ops:
  1.3 122.0 %layer.1 = (bf16[128,2048]{1,0:T(8,128)(2,1)}, bf16[128,2048]{1,0:T(8,128)(2,1)}, bf16[128,1024]{1,0:T(8,128)(2,1)}, bf16[64,2048]{1,0:T(8,128)(2,1)}) custom-call(bf16[128,2048]{1,0:T(8,128)(2,1)} %bitcast.21, bf16[128,2048]{1,0:T(8,128)(2,1)} %bitcast.22, s32[1,1]{1,0:T(1,128)S(6)} %copy.17.action_any, bf16[64,2048]{1,0:T(8,128)(2,1)} %table_any.1, ...), custom_call_target="tpu_custom_call" | custom-call | tf_op jit(solution)/shard_map/layer/pallas_call | solution.py:826
  123.3 2.2 %deliver.1 = (bf16[128,2048]{1,0:T(8,128)(2,1)}, bf16[128,2048]{1,0:T(8,128)(2,1)}, bf16[128,1024]{1,0:T(8,128)(2,1)}, bf16[64,2048]{1,0:T(8,128)(2,1)}) custom-call(bf16[128,2048]{1,0:T(8,128)(2,1)} %get-tuple-element.12.refs_0_, bf16[128,2048]{1,0:T(8,128)(2,1)} %get-tuple-element.13.refs_1_, bf16[128,1024]{1,0:T(8,128)(2,1)} %get-tuple-element.14.refs_2_, ...), custom_call_target="tpu_custom_call" | custom-call | tf_op jit(solution)/shard_map/deliver/pallas_call | solution.py:925

commit v4 on v3

--- a/solution.py
+++ b/solution.py
@@ -629,10 +629,7 @@
 
     down_weights(1 - core)
     pair_start(0)
-    turn(1)
     down_weights(core)
-    up_weights(1 - core)
-    pair_start(1)
 
     def send_rows(dst, product):
         rest = None
@@ -676,6 +673,9 @@
     pair_wait(0, near_chips)
     first_hop(0)
     first_hop(1)
+    turn(1)
+    up_weights(1 - core)
+    pair_start(1)
     up_weights(core)
     pair_wait(1, near_chips)
     first_hop(2)

time: 126 us -> 127 us (level)
  no operation moved by 1% of the time
where the time goes in v4:
time: 127 us
  Pallas kernels  125 us (98%)
  between operations  1.45 us (1%)
    pallas_call x1, Pallas kernels, local(): pl.pallas_call(layer_kernel, out_shape=results, in_specs=[hbm] * 13, out_...  123 us

profile of v4, /device:TPU:1, one launch (start us, length us, event | category | flops | bytes accessed | tf_op | source)
XLA Modules:
  0.0 126.6 jit_solution(5480856047741374085)
XLA Ops:
  1.3 122.9 %layer.1 = (bf16[128,2048]{1,0:T(8,128)(2,1)}, bf16[128,2048]{1,0:T(8,128)(2,1)}, bf16[128,1024]{1,0:T(8,128)(2,1)}, bf16[64,2048]{1,0:T(8,128)(2,1)}) custom-call(bf16[128,2048]{1,0:T(8,128)(2,1)} %bitcast.21, bf16[128,2048]{1,0:T(8,128)(2,1)} %bitcast.22, s32[1,1]{1,0:T(1,128)S(6)} %copy.17.action_any, bf16[64,2048]{1,0:T(8,128)(2,1)} %table_any.1, ...), custom_call_target="tpu_custom_call" | custom-call | tf_op jit(solution)/shard_map/layer/pallas_call | solution.py:826
  124.2 2.2 %deliver.1 = (bf16[128,2048]{1,0:T(8,128)(2,1)}, bf16[128,2048]{1,0:T(8,128)(2,1)}, bf16[128,1024]{1,0:T(8,128)(2,1)}, bf16[64,2048]{1,0:T(8,128)(2,1)}) custom-call(bf16[128,2048]{1,0:T(8,128)(2,1)} %get-tuple-element.12.refs_0_, bf16[128,2048]{1,0:T(8,128)(2,1)} %get-tuple-element.13.refs_1_, bf16[128,1024]{1,0:T(8,128)(2,1)} %get-tuple-element.14.refs_2_, ...), custom_call_target="tpu_custom_call" | custom-call | tf_op jit(solution)/shard_map/deliver/pallas_call | solution.py:925
